TPU v7x, 128 devices: a whole 4x4x4 slice. The times are simulated.
128 devices in a mesh: dp: 32 (over x, y, z_lo), tensor: 4 (over z_hi, core).
Axes of the slice: x: 4, y: 4, z: 4 (z_hi: 2, z_lo: 2; z = z_hi * 2 + z_lo), core: 2. Of those that a mesh axis runs over, the one named last changes fastest.
Arguments:
- tokens: bfloat16 [16384, 1536], P('dp'), may hold values from -6 to 6
- segments: int32 [32, 512], P('dp'), may hold values from 0 to 3, never falling along the last dimension, each value on 1 to 384 neighbouring positions
- norm_one: float32 [1536], replicated, may hold values from 0.1 to 1.9
- w_query: bfloat16 [1536, 1536], P(None, 'tensor'), may hold values from -0.15625 to 0.15625
- key_projection: bfloat16 [1536, 512], P(None, 'tensor'), may hold values from -0.15625 to 0.15625
- value_projection: bfloat16 [1536, 512], P(None, 'tensor'), may hold values from -0.15625 to 0.15625
- w_out: bfloat16 [1536, 1536], P('tensor'), may hold values from -0.625 to 0.625
- q_gain: float32 [64], replicated, may hold values from 0.1 to 1.9
- k_gain: float32 [64], replicated, may hold values from 0.1 to 1.9
- norm_two: float32 [1536], replicated, may hold values from 0.1 to 1.9
- w_gate: bfloat16 [1536, 6912], P(None, 'tensor'), may hold values from -0.15625 to 0.15625
- w_up: bfloat16 [1536, 6912], P(None, 'tensor'), may hold values from -0.15625 to 0.15625
- w_down: bfloat16 [6912, 1536], P('tensor'), may hold values from -0.078125 to 0.078125
- cotangent: bfloat16 [16384, 1536], P('dp'), may hold values from -6 to 6
Outputs:
- block_out: bfloat16 [16384, 1536], P('dp')
- grad_tokens: bfloat16 [16384, 1536], P('dp')
- grad_norm_one: float32 [1536], P('dp')
- grad_query: float32 [1536, 1536], P('dp', 'tensor')
- grad_key: float32 [1536, 512], P('dp', 'tensor')
- grad_value: float32 [1536, 512], P('dp', 'tensor')
- grad_out: float32 [1536, 1536], P('tensor', 'dp')
- grad_q_gain: float32 [64], replicated
- grad_k_gain: float32 [64], replicated
- grad_norm_two: float32 [1536], P('dp')
- grad_gate: float32 [1536, 6912], P('dp', 'tensor')
- grad_up: float32 [1536, 6912], P('dp', 'tensor')
- grad_down: float32 [6912, 1536], P('tensor', 'dp')
Inputs may be any that keep to these rules, and one draw needn't show every extreme that they name: `segments`: within a row document numbers never fall; a document holds 1 to 384 tokens of its row, and some holds exactly that many.
All inputs are finite; a program needn't handle non-finite values.
Results may differ from a plain program's by a relative error of at most 0.014.
Values sent between devices are 32-bit elements; how exact they have to be, the bound alone decides.
A program may use at most 192 MiB of HBM per device.

v0:
```python
import jax
import jax.numpy as jnp
from jax import lax
from jax.sharding import PartitionSpec as P

QUERY_HEADS = 24
KEY_VALUE_HEADS = 8
HEAD_SIZE = 64


EPSILON = 1e-05
THETA = 1000000.0


def rope_tables(segments):
    sequence_count, sequence_length = segments.shape
    index_row = jnp.arange(sequence_length, dtype=jnp.int32)[None, :]
    change = jnp.concatenate(
        [jnp.ones((sequence_count, 1), jnp.bool_), segments[:, 1:] != segments[:, :-1]], axis=1
    )
    starts = lax.cummax(jnp.where(change, index_row, 0), axis=1)
    position = (index_row - starts).astype(jnp.float32)
    frequency = THETA ** (-jnp.arange(HEAD_SIZE // 2, dtype=jnp.float32) * 2.0 / HEAD_SIZE)
    angles = position[:, :, None] * frequency
    allowed = (segments[:, :, None] == segments[:, None, :]) & (
        index_row[:, :, None] >= index_row[:, None, :]
    )
    return (jnp.cos(angles), jnp.sin(angles), allowed)


def apply_rotary(values, cosine_table, sine_table):
    first, second = jnp.split(values, 2, axis=-1)
    return jnp.concatenate(
        [first * cosine_table - second * sine_table, second * cosine_table + first * sine_table],
        axis=-1,
    )


def rotate_back(upstream, cosine_table, sine_table):
    first, second = jnp.split(upstream, 2, axis=-1)
    return jnp.concatenate(
        [first * cosine_table + second * sine_table, second * cosine_table - first * sine_table],
        axis=-1,
    )


def norm_rows(values, gain):
    inverse = lax.rsqrt(jnp.mean(values * values, axis=-1, keepdims=True) + EPSILON)
    return (values * inverse * gain, inverse)


def norm_back(values, inverse, gain, upstream):
    scaled = upstream * gain
    grad_in = inverse * scaled - values * inverse**3 * jnp.mean(
        scaled * values, axis=-1, keepdims=True
    )
    gain_grad = jnp.sum((upstream * values * inverse).reshape(-1, values.shape[-1]), axis=0)
    return (grad_in, gain_grad)


def per_device(
    tokens,
    segments,
    norm_one,
    w_query,
    key_projection,
    value_projection,
    w_out,
    q_gain,
    k_gain,
    norm_two,
    w_gate,
    w_up,
    w_down,
    cotangent,
):
    sequence_count, sequence_length = segments.shape
    token_count = tokens.shape[0]
    heads_local = w_query.shape[1] // HEAD_SIZE
    groups_local = key_projection.shape[1] // HEAD_SIZE
    group_count = QUERY_HEADS // KEY_VALUE_HEADS
    scale = HEAD_SIZE ** (-0.5)
    cosine_table, sine_table, allowed = rope_tables(segments)
    cosine_table = cosine_table[:, :, None, :]
    sine_table = sine_table[:, :, None, :]
    mask_full = allowed[:, None, None]
    tokens_f = tokens.astype(jnp.float32)
    first_hidden, inv_one = norm_rows(tokens_f, norm_one)
    hidden_one_low = first_hidden.astype(jnp.bfloat16)
    query_unrotated = jnp.dot(hidden_one_low, w_query, preferred_element_type=jnp.float32).reshape(
        sequence_count, sequence_length, heads_local, HEAD_SIZE
    )
    key_unrotated = jnp.dot(
        hidden_one_low, key_projection, preferred_element_type=jnp.float32
    ).reshape(sequence_count, sequence_length, groups_local, HEAD_SIZE)
    value_low = (
        jnp.dot(hidden_one_low, value_projection, preferred_element_type=jnp.float32)
        .astype(jnp.bfloat16)
        .reshape(sequence_count, sequence_length, groups_local, HEAD_SIZE)
    )
    query_norm, query_inv = norm_rows(query_unrotated, q_gain)
    key_norm, key_inv = norm_rows(key_unrotated, k_gain)
    query_low = (
        apply_rotary(query_norm, cosine_table, sine_table)
        .astype(jnp.bfloat16)
        .reshape(sequence_count, sequence_length, groups_local, group_count, HEAD_SIZE)
    )
    key_low = apply_rotary(key_norm, cosine_table, sine_table).astype(jnp.bfloat16)
    scores = (
        jnp.einsum("sqhgd,skhd->shgqk", query_low, key_low, preferred_element_type=jnp.float32)
        * scale
    )
    scores = jnp.where(mask_full, scores, -1e30)
    highest = jnp.max(scores, axis=-1, keepdims=True)
    expo_scores = jnp.exp(scores - highest)
    probs = expo_scores / jnp.sum(expo_scores, axis=-1, keepdims=True)
    probs_low = probs.astype(jnp.bfloat16)
    mixed = jnp.einsum(
        "shgqk,skhd->sqhgd", probs_low, value_low, preferred_element_type=jnp.float32
    )
    mixed_low = mixed.reshape(token_count, heads_local * HEAD_SIZE).astype(jnp.bfloat16)
    attn_part = jnp.dot(mixed_low, w_out, preferred_element_type=jnp.float32)
    attention = lax.psum(attn_part, "tensor")
    resid = tokens_f + attention
    hidden_two, inv_two = norm_rows(resid, norm_two)
    hidden_two_low = hidden_two.astype(jnp.bfloat16)
    gate = jnp.dot(hidden_two_low, w_gate, preferred_element_type=jnp.float32)
    upper = jnp.dot(hidden_two_low, w_up, preferred_element_type=jnp.float32)
    sigmoid_gate = jax.nn.sigmoid(gate)
    silu_gate = gate * sigmoid_gate
    activ_low = (silu_gate * upper).astype(jnp.bfloat16)
    ffn_part = jnp.dot(activ_low, w_down, preferred_element_type=jnp.float32)
    feed = lax.psum(ffn_part, "tensor")
    block_out = (resid + feed).astype(jnp.bfloat16)
    grad_y = cotangent.astype(jnp.float32)
    grad_down = jnp.einsum("tf,td->fd", activ_low, cotangent, preferred_element_type=jnp.float32)
    grad_activ = jnp.einsum("td,fd->tf", cotangent, w_down, preferred_element_type=jnp.float32)
    grad_gate_in = (grad_activ * upper * sigmoid_gate * (1.0 + gate * (1.0 - sigmoid_gate))).astype(
        jnp.bfloat16
    )
    grad_up_in = (grad_activ * silu_gate).astype(jnp.bfloat16)
    grad_gate = jnp.einsum(
        "td,tf->df", hidden_two_low, grad_gate_in, preferred_element_type=jnp.float32
    )
    grad_up = jnp.einsum(
        "td,tf->df", hidden_two_low, grad_up_in, preferred_element_type=jnp.float32
    )
    hidden_two_part = jnp.einsum(
        "tf,df->td", grad_gate_in, w_gate, preferred_element_type=jnp.float32
    ) + jnp.einsum("tf,df->td", grad_up_in, w_up, preferred_element_type=jnp.float32)
    grad_hidden_two = lax.psum(hidden_two_part, "tensor")
    resid_back, grad_norm_two = norm_back(resid, inv_two, norm_two, grad_hidden_two)
    grad_resid = grad_y + resid_back
    grad_attn_low = grad_resid.astype(jnp.bfloat16)
    grad_out = jnp.einsum("ta,td->ad", mixed_low, grad_attn_low, preferred_element_type=jnp.float32)
    grad_mixed = jnp.einsum("td,ad->ta", grad_attn_low, w_out, preferred_element_type=jnp.float32)
    grad_mixed_low = grad_mixed.astype(jnp.bfloat16).reshape(
        sequence_count, sequence_length, groups_local, group_count, HEAD_SIZE
    )
    grad_probs = jnp.einsum(
        "sqhgd,skhd->shgqk", grad_mixed_low, value_low, preferred_element_type=jnp.float32
    )
    grad_values = jnp.einsum(
        "shgqk,sqhgd->skhd", probs_low, grad_mixed_low, preferred_element_type=jnp.float32
    )
    grad_values_low = grad_values.reshape(token_count, groups_local * HEAD_SIZE).astype(
        jnp.bfloat16
    )
    grad_scores = probs * (grad_probs - jnp.sum(probs * grad_probs, axis=-1, keepdims=True))
    grad_scores_low = grad_scores.astype(jnp.bfloat16)
    grad_query_rot = (
        jnp.einsum(
            "shgqk,skhd->sqhgd", grad_scores_low, key_low, preferred_element_type=jnp.float32
        )
        * scale
    )
    grad_key_rot = (
        jnp.einsum(
            "shgqk,sqhgd->skhd", grad_scores_low, query_low, preferred_element_type=jnp.float32
        )
        * scale
    )
    grad_query_norm = rotate_back(
        grad_query_rot.reshape(sequence_count, sequence_length, heads_local, HEAD_SIZE),
        cosine_table,
        sine_table,
    )
    grad_key_norm = rotate_back(grad_key_rot, cosine_table, sine_table)
    grad_query_raw, grad_q_part = norm_back(query_unrotated, query_inv, q_gain, grad_query_norm)
    grad_key_raw, grad_k_part = norm_back(key_unrotated, key_inv, k_gain, grad_key_norm)
    grad_query_low = grad_query_raw.reshape(token_count, heads_local * HEAD_SIZE).astype(
        jnp.bfloat16
    )
    grad_key_low = grad_key_raw.reshape(token_count, groups_local * HEAD_SIZE).astype(jnp.bfloat16)
    grad_query = jnp.einsum(
        "td,tc->dc", hidden_one_low, grad_query_low, preferred_element_type=jnp.float32
    )
    grad_key = jnp.einsum(
        "td,tc->dc", hidden_one_low, grad_key_low, preferred_element_type=jnp.float32
    )
    grad_value = jnp.einsum(
        "td,tc->dc", hidden_one_low, grad_values_low, preferred_element_type=jnp.float32
    )
    hidden_one_part = (
        jnp.einsum("tc,dc->td", grad_query_low, w_query, preferred_element_type=jnp.float32)
        + jnp.einsum("tc,dc->td", grad_key_low, key_projection, preferred_element_type=jnp.float32)
        + jnp.einsum(
            "tc,dc->td", grad_values_low, value_projection, preferred_element_type=jnp.float32
        )
    )
    grad_hidden_one = lax.psum(hidden_one_part, "tensor")
    tokens_back, grad_norm_one = norm_back(tokens_f, inv_one, norm_one, grad_hidden_one)
    grad_tokens = (grad_resid + tokens_back).astype(jnp.bfloat16)
    (
        grad_query_sh,
        grad_key_sh,
        grad_value_sh,
        grad_out_sh,
        grad_norm_one_sh,
        grad_gate_sh,
        grad_up_sh,
        grad_down_sh,
        grad_norm_two_sh,
    ) = (
        lax.psum_scatter(grad_query, "dp", scatter_dimension=0, tiled=True),
        lax.psum_scatter(grad_key, "dp", scatter_dimension=0, tiled=True),
        lax.psum_scatter(grad_value, "dp", scatter_dimension=0, tiled=True),
        lax.psum_scatter(grad_out, "dp", scatter_dimension=1, tiled=True),
        lax.psum_scatter(grad_norm_one, "dp", scatter_dimension=0, tiled=True),
        lax.psum_scatter(grad_gate, "dp", scatter_dimension=0, tiled=True),
        lax.psum_scatter(grad_up, "dp", scatter_dimension=0, tiled=True),
        lax.psum_scatter(grad_down, "dp", scatter_dimension=1, tiled=True),
        lax.psum_scatter(grad_norm_two, "dp", scatter_dimension=0, tiled=True),
    )
    grad_q_gain, grad_k_gain = lax.psum((grad_q_part, grad_k_part), ("dp", "tensor"))
    return (
        block_out,
        grad_tokens,
        grad_norm_one_sh,
        grad_query_sh,
        grad_key_sh,
        grad_value_sh,
        grad_out_sh,
        grad_q_gain,
        grad_k_gain,
        grad_norm_two_sh,
        grad_gate_sh,
        grad_up_sh,
        grad_down_sh,
    )


def solution(mesh):
    placed = (
        P("dp", None),
        P("dp", None),
        P(),
        P(None, "tensor"),
        P(None, "tensor"),
        P(None, "tensor"),
        P("tensor", None),
        P(),
        P(),
        P(),
        P(None, "tensor"),
        P(None, "tensor"),
        P("tensor", None),
        P("dp", None),
    )
    return jax.shard_map(
        per_device,
        mesh=mesh,
        in_specs=placed,
        out_specs=(
            P("dp", None),
            P("dp", None),
            P("dp"),
            P("dp", "tensor"),
            P("dp", "tensor"),
            P("dp", "tensor"),
            P("tensor", "dp"),
            P(),
            P(),
            P("dp"),
            P("dp", "tensor"),
            P("dp", "tensor"),
            P("tensor", "dp"),
        ),
        check_vma=False,
    )
```

profile of v0, /device:TPU:0, one launch (start us, length us, event | category | flops | bytes accessed | tf_op | source)
XLA Modules:
  0.0 1757.3 jit_solution(8767335514996641334)
XLA Ops:
  32.3 2.7 fusion.60
  35.6 78.1 %all-reduce.9.cloned.1.call-done = f32[512,1536]{1,0:T(8,128)} async-done(((f32[512,1536]{1,0:T(8,128)}), f32[512,1536]{1,0:T(8,128)}) %all-reduce.9.cloned.1.call-update) | async-done | bytes 3145744 | tf_op jit(solution)/shard_map/psum | solution.py:123
  113.7 2.8 multiply_reduce_fusion.2
  118.5 5.7 fusion.61
  124.2 4.9 fusion.62
  129.2 7.1 multiply_convert_fusion
  136.3 3.1 fusion.64
  139.4 5.0 convolution_add_fusion.2
  149.5 7.9 fusion.63
  157.4 62.3 %all-reduce.11.cloned.1.call-done = f32[512,1536]{1,0:T(8,128)} async-done(((f32[512,1536]{1,0:T(8,128)}), f32[512,1536]{1,0:T(8,128)}) %all-reduce.11.cloned.1.call-update) | async-done | bytes 3145744 | tf_op jit(solution)/shard_map/psum | solution.py:151
  219.7 4.4 multiply_reduce_fusion
  224.1 3.4 subtract_add_fusion
  228.8 2.3 fusion
  231.1 2.2 fusion.7
  241.1 2.2 convolution_add_fusion
  247.4 2.5 fusion.66
  250.0 5.1 fusion.40
  255.2 7.4 fusion.69
  262.6 7.6 fusion.70
  271.6 7.3 fusion.71
  289.1 2.6 concatenate.91
  292.2 3.5 fusion.24
  295.6 91.6 %all-reduce.2 = (f32[64]{0:T(128)}, f32[64]{0:T(128)}) all-reduce(f32[64]{0:T(128)S(1)} %fusion.24, f32[64]{0:T(128)S(1)} %fusion.44), channel_id=1, replica_groups=mesh['dp'=32,'tensor'=4] {'dp','tensor'}, use_global_device_ids=true, to_apply=%region_24.25 | all-reduce | flops 128 | bytes 1024 | tf_op jit(solution)/shard_map/psum | solution.py:235
  387.2 2.9 fusion.17
  390.1 154.2 %all-reduce.3 = (f32[1536]{0:T(1024)S(1)}, f32[1536]{0:T(1024)S(1)}) all-reduce(f32[1536]{0:T(1024)S(1)} %get-tuple-element.15, f32[1536]{0:T(1024)S(1)} %copy-done.61), channel_id=2, replica_groups=mesh['dp'=32,'tensor'=4] {'dp'}, use_global_device_ids=true, to_apply=%region_18.19.clone | all-reduce | flops 3072 | bytes 24576
  545.5 7.0 fusion.14
  552.5 140.4 %reduce-scatter.10.cloned.1.call-done = f32[48,128]{1,0:T(8,128)} async-done(((f32[1536,128]{1,0:T(8,128)}), f32[48,128]{1,0:T(8,128)}) %reduce-scatter.10.cloned.1.call-update) | async-done | bytes 24592 | tf_op jit(solution)/shard_map/reduce_scatter | solution.py:226
  692.9 162.5 %reduce-scatter.8.cloned.1.call-done = f32[48,384]{1,0:T(8,128)} async-done(((f32[1536,384]{1,0:T(8,128)}), f32[48,384]{1,0:T(8,128)}) %reduce-scatter.8.cloned.1.call-update) | async-done | bytes 73744 | tf_op jit(solution)/shard_map/reduce_scatter | solution.py:225
  855.4 163.9 %reduce-scatter.14.cloned.1.call-done = f32[384,48]{0,1:T(8,128)} async-done(((f32[384,1536]{0,1:T(8,128)}), f32[384,48]{0,1:T(8,128)}) %reduce-scatter.14.cloned.1.call-update) | async-done | bytes 73744 | tf_op jit(solution)/shard_map/reduce_scatter | solution.py:228
  1019.2 241.2 %reduce-scatter.16.cloned.1.call-done = f32[48,1728]{1,0:T(8,128)} async-done(((f32[1536,1728]{1,0:T(8,128)}), f32[48,1728]{1,0:T(8,128)}) %reduce-scatter.16.cloned.1.call-update) | async-done | bytes 331792 | tf_op jit(solution)/shard_map/reduce_scatter | solution.py:230
  1260.5 245.4 %reduce-scatter.18.cloned.1.call-done = f32[48,1728]{1,0:T(8,128)} async-done(((f32[1536,1728]{1,0:T(8,128)}), f32[48,1728]{1,0:T(8,128)}) %reduce-scatter.18.cloned.1.call-update) | async-done | bytes 331792 | tf_op jit(solution)/shard_map/reduce_scatter | solution.py:231
  1505.9 244.1 %reduce-scatter.20.cloned.1.call-done = f32[1728,48]{0,1:T(8,128)} async-done(((f32[1728,1536]{0,1:T(8,128)}), f32[1728,48]{0,1:T(8,128)}) %reduce-scatter.20.cloned.1.call-update) | async-done | bytes 331792 | tf_op jit(solution)/shard_map/reduce_scatter | solution.py:232
  (264 shorter events, 57.8 us)
Async XLA Ops:
  7.2 25.2 %copy-start = (bf16[384,1536]{1,0:T(8,128)(2,1)S(1)}, bf16[384,1536]{1,0:T(8,128)(2,1)}, u32[]{:S(2)}) copy-start(bf16[384,1536]{1,0:T(8,128)(2,1)} %param.20) | copy-start | bytes 3538948
  7.2 106.5 %all-reduce.9.cloned.1.call-start = ((), (), s32[]{:S(2)}) async-start(), calls=%async_computation.7 | async-start | bytes 6291456 | tf_op jit(solution)/shard_map/psum | solution.py:123
  7.2 5.3 copy-start.37
  19.2 5.0 copy-start.70
  35.1 184.6 %all-reduce.11.cloned.1.call-start = ((), (), s32[]{:S(2)}) async-start(), calls=%async_computation.8 | async-start | bytes 6291456 | tf_op jit(solution)/shard_map/psum | solution.py:151
  116.5 7.6 copy-start.2
  118.1 6.1 slice-start.2
  118.1 11.0 slice-start.6
  118.5 5.7 copy-start.28
  118.5 5.7 slice-start.3
  118.5 10.7 slice-start.7
  124.2 4.9 copy-start.26
  124.2 12.1 slice-start.4
  129.1 7.1 slice-start.5
  144.4 242.8 %all-reduce.13.cloned.1.call-start = ((), (), s32[]{:S(2)}) async-start(), calls=%async_computation.16 | async-start | bytes 12582912 | tf_op jit(solution)/shard_map/psum | solution.py:133
  219.7 8.6 slice-start
  243.4 309.1 %reduce-scatter.12.cloned.1.call-start = ((), (), s32[]{:S(2)}) async-start(), calls=%async_computation.11 | async-start | bytes 811008 | tf_op jit(solution)/shard_map/reduce_scatter | solution.py:227
  245.8 447.1 %reduce-scatter.10.cloned.1.call-start = ((), (), s32[]{:S(2)}) async-start(), calls=%async_computation.10 | async-start | bytes 811008 | tf_op jit(solution)/shard_map/reduce_scatter | solution.py:226
  247.4 608.0 %reduce-scatter.8.cloned.1.call-start = ((), (), s32[]{:S(2)}) async-start(), calls=%async_computation.9 | async-start | bytes 2433024 | tf_op jit(solution)/shard_map/reduce_scatter | solution.py:225
  249.9 5.2 copy-start.29
  249.9 769.3 %reduce-scatter.14.cloned.1.call-start = ((), (), s32[]{:S(2)}) async-start(), calls=%async_computation.12 | async-start | bytes 2433024 | tf_op jit(solution)/shard_map/reduce_scatter | solution.py:228
  255.1 1005.4 %reduce-scatter.16.cloned.1.call-start = ((), (), s32[]{:S(2)}) async-start(), calls=%async_computation.13 | async-start | bytes 11354112 | tf_op jit(solution)/shard_map/reduce_scatter | solution.py:230
  262.6 1243.3 %reduce-scatter.18.cloned.1.call-start = ((), (), s32[]{:S(2)}) async-start(), calls=%async_computation.14 | async-start | bytes 11354112 | tf_op jit(solution)/shard_map/reduce_scatter | solution.py:231
  270.3 1479.8 %reduce-scatter.20.cloned.1.call-start = ((), (), s32[]{:S(2)}) async-start(), calls=%async_computation.15 | async-start | bytes 11354112 | tf_op jit(solution)/shard_map/reduce_scatter | solution.py:232
  279.0 4.7 copy-start.36
  279.4 5.5 copy-start.13
  291.8 95.4 %copy-start.5 = (bf16[512,1536]{1,0:T(8,128)(2,1)S(1)}, bf16[512,1536]{1,0:T(8,128)(2,1)}, u32[]{:S(2)}) copy-start(bf16[512,1536]{1,0:T(8,128)(2,1)} %param.14) | copy-start | bytes 4718596
  291.8 95.4 %copy-start.52 = (f32[1536]{0:T(1024)S(1)}, f32[1536]{0:T(1024)}, u32[]{:S(2)}) copy-start(f32[1536]{0:T(1024)} %param.16) | copy-start | bytes 18436
  291.8 95.4 %copy-start.65 = (f32[512]{0:T(512)S(1)}, f32[512]{0:T(512)}, u32[]{:S(2)}) copy-start(f32[512]{0:T(512)} %copy-done.64) | copy-start | bytes 6148
  295.6 94.5 %copy-start.61 = (f32[1536]{0:T(1024)S(1)}, f32[1536]{0:T(1024)}, u32[]{:S(2)}) copy-start(f32[1536]{0:T(1024)} %get-tuple-element.13) | copy-start | bytes 18436
  295.6 249.9 %copy-start.67 = (f32[512]{0:T(512)S(1)}, f32[512]{0:T(512)}, u32[]{:S(2)}) copy-start(f32[512]{0:T(512)} %get-tuple-element.46) | copy-start | bytes 6148
  545.5 1204.5 %copy-start.1 = (bf16[384,1536]{1,0:T(8,128)(2,1)S(1)}, bf16[384,1536]{1,0:T(8,128)(2,1)}, u32[]{:S(2)}) copy-start(bf16[384,1536]{1,0:T(8,128)(2,1)} %param.20) | copy-start | bytes 3538948
  (62 other events, 140.6 us)
Sparse Core Ops, SparseCore 0:
  35.2 78.4 all-reduce.8
  144.5 75.1 all-reduce.10
  243.5 127.3 all-reduce.12
  373.7 159.7 reduce-scatter.11
  536.4 156.4 reduce-scatter.9
  695.7 159.6 reduce-scatter.7
  858.3 160.8 reduce-scatter.13
  1022.2 238.2 reduce-scatter.15
  1263.6 242.2 reduce-scatter.17
  1508.7 241.2 reduce-scatter.19
where the time goes:
time: 1760 us
  waiting for transfers between devices  1340 us (76%)
  blocking collectives  246 us (14%)
  matrix products  86.1 us (5%)
  other arithmetic  41.6 us (2%)
  local copies, waits for them, and re-layouts  28.3 us (2%)
    reduce_scatter x1, waiting for transfers between devices, per_device(): lax.psum_scatter(grad_up, 'dp', scatter_dimension=0, tiled=True)  245 us
    reduce_scatter x1, waiting for transfers between devices, per_device(): lax.psum_scatter(grad_down, 'dp', scatter_dimension=1, tiled=True)  244 us
    reduce_scatter x1, waiting for transfers between devices, per_device(): lax.psum_scatter(grad_gate, 'dp', scatter_dimension=0, tiled=True)  241 us
    reduce_scatter x1, waiting for transfers between devices, per_device(): lax.psum_scatter(grad_out, 'dp', scatter_dimension=1, tiled=True)  164 us
    reduce_scatter x1, waiting for transfers between devices, per_device(): lax.psum_scatter(grad_query, 'dp', scatter_dimension=0, tiled=True)  162 us
    unnamed x1, blocking collectives  154 us
    reduce_scatter x1, waiting for transfers between devices, per_device(): lax.psum_scatter(grad_key, 'dp', scatter_dimension=0, tiled=True)  140 us
    psum x1, blocking collectives, per_device(): lax.psum((grad_q_part, grad_k_part), ('dp', 'tensor'))  91.6 us
  transfers between devices with their start and end apart: 10, of which 8 were waited for; matrix products, arithmetic and copies ran while one was open for 4% of the time, Pallas kernels for 0%

commit v1 on v0

--- a/solution.py
+++ b/solution.py
@@ -1,6 +1,8 @@
 import jax
 import jax.numpy as jnp
 from jax import lax
+from jax.experimental import pallas as pl
+from jax.experimental.pallas import tpu as pltpu
 from jax.sharding import PartitionSpec as P
 
 QUERY_HEADS = 24
@@ -56,6 +58,710 @@
     )
     gain_grad = jnp.sum((upstream * values * inverse).reshape(-1, values.shape[-1]), axis=0)
     return (grad_in, gain_grad)
+
+
+MESH = pl.DeviceIdType.MESH
+F32 = jnp.float32
+BF16 = jnp.bfloat16
+WIDTH = 1536
+TOK = 512
+HALF = 256
+FFL = 1728
+MIB = 1 << 20
+
+
+def place():
+    dp = lax.axis_index("dp")
+    tensor = lax.axis_index("tensor")
+    x = lax.div(dp, 8)
+    y = lax.rem(lax.div(dp, 2), 4)
+    z = lax.div(tensor, 2) * 2 + lax.rem(dp, 2)
+    return x, y, z, lax.rem(tensor, 2)
+
+
+def device(x, y, z, core):
+    return (x * 8 + y * 2 + lax.rem(z, 2), lax.div(z, 2) * 2 + core)
+
+
+def greet(partners):
+    barrier = pltpu.get_barrier_semaphore()
+    for partner in partners:
+        pl.semaphore_signal(barrier, inc=1, device_id=partner, device_id_type=MESH)
+    pl.semaphore_wait(barrier, len(partners))
+
+
+def remote(source, target, send_sem, recv_sem, partner):
+    return pltpu.make_async_remote_copy(
+        src_ref=source,
+        dst_ref=target,
+        send_sem=send_sem,
+        recv_sem=recv_sem,
+        device_id=partner,
+        device_id_type=MESH,
+    )
+
+
+def by_rows(count, step, work):
+    def body(i, carry):
+        work(pl.ds(pl.multiple_of(i * step, step), step))
+        return carry
+
+    lax.fori_loop(0, count // step, body, 0)
+
+
+PARTS = 4
+PART = HALF // PARTS
+
+
+def start_norm_kernel(
+    part, tokens, gain, x1_out, h2_out, own, near, far, back, fin, sems, near_s, near_r, far_s, far_r, back_s, back_r
+):
+    x, y, z, core = place()
+    mate = device(x, y, z, 1 - core)
+    across = device(x, y, lax.rem(z + 2, 4), core)
+    greet([mate, across])
+    load = pltpu.make_async_copy(part.at[core], own, sems)
+    load.start()
+    first, second, third = [], [], []
+    for j in range(PARTS):
+        rows = pl.ds(j * PART, PART)
+        copy = remote(part.at[1 - core, rows], near.at[rows], near_s.at[j], near_r.at[j], mate)
+        copy.start()
+        first.append(copy)
+    load.wait()
+    for j in range(PARTS):
+        rows = pl.ds(j * PART, PART)
+        first[j].wait_recv()
+
+        def add(r, j=j):
+            r = pl.ds(r.start + j * PART, r.size)
+            own[r] = own[r] + near[r]
+
+        by_rows(PART, 16, add)
+        copy = remote(own.at[rows], far.at[rows], far_s.at[j], far_r.at[j], across)
+        copy.start()
+        second.append(copy)
+    for j in range(PARTS):
+        rows = pl.ds(j * PART, PART)
+        second[j].wait_recv()
+
+        def norm(r, j=j):
+            r = pl.ds(pl.multiple_of(r.start + j * PART, 16), r.size)
+            value = tokens[core, r].astype(F32) + (own[r] + far[r])
+            inverse = lax.rsqrt(jnp.mean(value * value, axis=-1, keepdims=True) + EPSILON)
+            low = (value * inverse * gain[...]).astype(BF16)
+            x1_out[r] = value
+            h2_out[core, r] = low
+            fin[r] = low.astype(F32)
+
+        by_rows(PART, 16, norm)
+        copy = remote(fin.at[rows], back.at[rows], back_s.at[j], back_r.at[j], mate)
+        copy.start()
+        third.append(copy)
+    for j in range(PARTS):
+        third[j].wait_recv()
+
+        def keep(r, j=j):
+            r = pl.ds(pl.multiple_of(r.start + j * PART, 16), r.size)
+            h2_out[1 - core, r] = back[r].astype(BF16)
+
+        by_rows(PART, 16, keep)
+    for copy in first + second + third:
+        copy.wait_send()
+
+
+def sum_scratch():
+    return [pltpu.VMEM((HALF, WIDTH), F32)] * 5 + [pltpu.SemaphoreType.DMA] + [
+        pltpu.SemaphoreType.DMA((PARTS,))
+    ] * 6
+
+
+def attention_sum(part, tokens, gain):
+    vmem = pl.BlockSpec(memory_space=pltpu.VMEM)
+    x1, h2 = pl.pallas_call(
+        start_norm_kernel,
+        out_shape=(
+            jax.ShapeDtypeStruct((HALF, WIDTH), F32),
+            jax.ShapeDtypeStruct((2, HALF, WIDTH), BF16),
+        ),
+        in_specs=[pl.BlockSpec(memory_space=pl.ANY), vmem, vmem],
+        out_specs=(vmem, vmem),
+        scratch_shapes=sum_scratch(),
+        compiler_params=pltpu.CompilerParams(
+            collective_id=1, has_side_effects=True, vmem_limit_bytes=40 * MIB
+        ),
+        name="attention_sum",
+    )(part.reshape(2, HALF, WIDTH), tokens.reshape(2, HALF, WIDTH), gain.reshape(1, WIDTH))
+    return x1, h2.reshape(TOK, WIDTH)
+
+
+def back_norm_kernel(
+    part, x1, upstream, gain, dx1_out, da_out, dg_out, own, near, far, back, fin, sems, near_s, near_r, far_s, far_r, back_s, back_r
+):
+    x, y, z, core = place()
+    mate = device(x, y, z, 1 - core)
+    across = device(x, y, lax.rem(z + 2, 4), core)
+    greet([mate, across])
+    load = pltpu.make_async_copy(part.at[core], own, sems)
+    load.start()
+    first, second, third = [], [], []
+    for j in range(PARTS):
+        rows = pl.ds(j * PART, PART)
+        copy = remote(part.at[1 - core, rows], near.at[rows], near_s.at[j], near_r.at[j], mate)
+        copy.start()
+        first.append(copy)
+    dg_out[...] = jnp.zeros((8, WIDTH), F32)
+    load.wait()
+    for j in range(PARTS):
+        rows = pl.ds(j * PART, PART)
+        first[j].wait_recv()
+
+        def add(r, j=j):
+            r = pl.ds(r.start + j * PART, r.size)
+            own[r] = own[r] + near[r]
+
+        by_rows(PART, 16, add)
+        copy = remote(own.at[rows], far.at[rows], far_s.at[j], far_r.at[j], across)
+        copy.start()
+        second.append(copy)
+    for j in range(PARTS):
+        rows = pl.ds(j * PART, PART)
+        second[j].wait_recv()
+
+        def norm(r, j=j):
+            r = pl.ds(pl.multiple_of(r.start + j * PART, 16), r.size)
+            value = x1[r]
+            total = own[r] + far[r]
+            inverse = lax.rsqrt(jnp.mean(value * value, axis=-1, keepdims=True) + EPSILON)
+            scaled = total * gain[...]
+            grad = (
+                upstream[core, r].astype(F32)
+                + inverse * scaled
+                - value * inverse**3 * jnp.mean(scaled * value, axis=-1, keepdims=True)
+            )
+            dg = total * value * inverse
+            dg_out[...] += dg[0:8] + dg[8:16]
+            low = grad.astype(BF16)
+            dx1_out[r] = grad
+            da_out[core, r] = low
+            fin[r] = low.astype(F32)
+
+        by_rows(PART, 16, norm)
+        copy = remote(fin.at[rows], back.at[rows], back_s.at[j], back_r.at[j], mate)
+        copy.start()
+        third.append(copy)
+    for j in range(PARTS):
+        third[j].wait_recv()
+
+        def keep(r, j=j):
+            r = pl.ds(pl.multiple_of(r.start + j * PART, 16), r.size)
+            da_out[1 - core, r] = back[r].astype(BF16)
+
+        by_rows(PART, 16, keep)
+    for copy in first + second + third:
+        copy.wait_send()
+
+
+def hidden_sum(part, x1, cotangent, gain):
+    vmem = pl.BlockSpec(memory_space=pltpu.VMEM)
+    dx1, da, dg = pl.pallas_call(
+        back_norm_kernel,
+        out_shape=(
+            jax.ShapeDtypeStruct((HALF, WIDTH), F32),
+            jax.ShapeDtypeStruct((2, HALF, WIDTH), BF16),
+            jax.ShapeDtypeStruct((8, WIDTH), F32),
+        ),
+        in_specs=[pl.BlockSpec(memory_space=pl.ANY), vmem, vmem, vmem],
+        out_specs=(vmem, vmem, vmem),
+        scratch_shapes=sum_scratch(),
+        compiler_params=pltpu.CompilerParams(
+            collective_id=2, has_side_effects=True, vmem_limit_bytes=40 * MIB
+        ),
+        name="hidden_sum",
+    )(part.reshape(2, HALF, WIDTH), x1, cotangent.reshape(2, HALF, WIDTH), gain.reshape(1, WIDTH))
+    return dx1, da.reshape(TOK, WIDTH), dg
+
+
+CMAX = 896
+CHUNKS = (
+    (0, 0, 0, 896, 0),
+    (0, 0, 896, 896, 0),
+    (0, 0, 1792, 896, 0),
+    (0, 0, 2688, 768, 0),
+    (1, 1, 0, 640, 1),
+    (2, 2, 0, 384, 2),
+    (3, 3, 0, 896, 3),
+    (3, 3, 896, 896, 3),
+)
+WIDTHS = (3456, 640, 384, 1792)
+XP, XM, YP, YM = range(4)
+OPPOSITE = (XM, XP, YM, YP)
+
+
+def scatter_kernel(*refs):
+    lefts, rights, refs = refs[:4], refs[4:8], refs[8:]
+    ffn_part, dh1_part, x1, dx1, tokens, gain, small_in, refs = *refs[:7], refs[7:]
+    grads, block_out, grad_tokens, small_out, refs = refs[:4], refs[4], refs[5], refs[6], refs[7:]
+    left_buf, right_buf, product, got, passed, got2, keep, got3, refs = *refs[:8], refs[8:]
+    sum_own, sum_near, sum_far, sum_back, refs = *refs[:4], refs[4:]
+    small, small_got, refs = refs[0], refs[1], refs[2:]
+    left_sem, right_sem, s1, r1, s2, r2, s3, r3, credit, credit2, credit3, load_sem, sum_s, sum_r, small_s, small_r = refs
+
+    x, y, z, core = place()
+    around = (
+        device(lax.rem(x + 1, 4), y, z, core),
+        device(lax.rem(x + 3, 4), y, z, core),
+        device(x, lax.rem(y + 1, 4), z, core),
+        device(x, lax.rem(y + 3, 4), z, core),
+    )
+    z_lo = lax.rem(z, 2)
+    beside = device(x, y, z + 1 - 2 * z_lo, core)
+    mate = device(x, y, z, 1 - core)
+    across = device(x, y, lax.rem(z + 2, 4), core)
+    ring = (
+        [device(lax.rem(x + i, 4), y, z, core) for i in (1, 2, 3)],
+        [device(x, lax.rem(y + i, 4), z, core) for i in (1, 2, 3)],
+        [device(x, y, lax.rem(z + i, 4), core) for i in (1, 2, 3)],
+        [mate],
+    )
+    greet([one for group in ring for one in group])
+
+    count = len(CHUNKS)
+    place1, place2 = (x, y), (y, x)
+    forward1, backward1 = (around[XP], around[YP]), (around[XM], around[YM])
+    forward2, backward2 = (around[YP], around[XP]), (around[YM], around[XM])
+
+    left_order = []
+    for chunk in CHUNKS:
+        if chunk[0] not in left_order:
+            left_order.append(chunk[0])
+    left_copies = [
+        pltpu.make_async_copy(lefts[which], left_buf.at[i % 2], left_sem.at[i % 2])
+        for i, which in enumerate(left_order)
+    ]
+    right_copies = [
+        pltpu.make_async_copy(
+            rights[chunk[1]].at[:, pl.ds(chunk[2], chunk[3])],
+            right_buf.at[k % 2, :, pl.ds(0, chunk[3])],
+            right_sem.at[k % 2],
+        )
+        for k, chunk in enumerate(CHUNKS)
+    ]
+    left_at = [left_order.index(chunk[0]) for chunk in CHUNKS]
+
+    first, second, third = [], [], []
+    for k, chunk in enumerate(CHUNKS):
+        slot, cols = k % 2, pl.ds(0, chunk[3])
+        per1, per2, per3 = [], [], []
+        for o in range(2):
+            far_block = lax.rem(place1[o] + 2, 4)
+            after, before = lax.rem(place1[o] + 1, 4), lax.rem(place1[o] + 3, 4)
+            top, low = pl.ds(0, 96), pl.ds(96, 96)
+            plan = (
+                (far_block, top, forward1[o]),
+                (far_block, low, backward1[o]),
+                (after, low, forward1[o]),
+                (before, top, backward1[o]),
+                (after, top, forward1[o]),
+                (before, low, backward1[o]),
+            )
+            per1.append(
+                [
+                    remote(
+                        product.at[slot, o, block, rows, cols],
+                        got.at[slot, o, i, :, cols],
+                        s1.at[slot, o, i],
+                        r1.at[slot, o, i],
+                        partner,
+                    )
+                    for i, (block, rows, partner) in enumerate(plan)
+                ]
+            )
+            far_block = lax.rem(place2[o] + 2, 4)
+            after, before = lax.rem(place2[o] + 1, 4), lax.rem(place2[o] + 3, 4)
+            plan = (
+                (far_block, 0, forward2[o]),
+                (far_block, 1, backward2[o]),
+                (after, 1, forward2[o]),
+                (before, 0, backward2[o]),
+                (after, 0, forward2[o]),
+                (before, 1, backward2[o]),
+            )
+            per2.append(
+                [
+                    remote(
+                        passed.at[slot, o, block, half, :, cols],
+                        got2.at[slot, o, i, :, cols],
+                        s2.at[slot, o, i],
+                        r2.at[slot, o, i],
+                        partner,
+                    )
+                    for i, (block, half, partner) in enumerate(plan)
+                ]
+            )
+            per3.append(
+                remote(
+                    keep.at[slot, o, 1 - z_lo, :, cols],
+                    got3.at[slot, o, :, cols],
+                    s3.at[slot, o],
+                    r3.at[slot, o],
+                    beside,
+                )
+            )
+        first.append(per1)
+        second.append(per2)
+        third.append(per3)
+
+    def multiply(k):
+        slot, width = k % 2, CHUNKS[k][3]
+        right_copies[k].wait()
+        if k == 0 or left_at[k] != left_at[k - 1]:
+            left_copies[left_at[k]].wait()
+        if k + 1 < count:
+            right_copies[k + 1].start()
+        if (k == 0 or left_at[k] != left_at[k - 1]) and left_at[k] + 1 < len(left_order):
+            left_copies[left_at[k] + 1].start()
+        if k >= 2:
+            for o in range(2):
+                for copy in first[k - 2][o]:
+                    copy.wait_send()
+
+        def block(b, carry):
+            rows = pl.ds(pl.multiple_of(b * 384, 384), 384)
+            for at in range(0, width, 256):
+                size = min(256, width - at)
+                cols = pl.ds(at, size)
+                tile = jnp.dot(
+                    left_buf[left_at[k] % 2, rows, :],
+                    right_buf[slot, :, cols],
+                    preferred_element_type=F32,
+                )
+                for q in range(8):
+                    product[slot, 0, b, pl.ds(24 * q, 24), cols] = tile[48 * q : 48 * q + 24]
+                    to = pl.ds(pl.multiple_of(48 * b + 24 * (q % 2), 24), 24)
+                    product[slot, 1, q // 2, to, cols] = tile[48 * q + 24 : 48 * q + 48]
+            return carry
+
+        lax.fori_loop(0, 4, block, 0)
+        if k >= 2:
+            for d in range(4):
+                pl.semaphore_wait(credit.at[d], 1)
+        for o in range(2):
+            for i in range(4):
+                first[k][o][i].start()
+
+    def relay(k):
+        slot, width = k % 2, CHUNKS[k][3]
+        cols = pl.ds(0, width)
+        for o in range(2):
+            for i, shift, base in ((0, 1, 0), (1, 3, 96)):
+                first[k][o][i].wait_recv()
+                b = lax.rem(place1[o] + shift, 4)
+
+                def add(r, o=o, i=i, b=b, base=base):
+                    to = pl.ds(pl.multiple_of(r.start + base, 8), r.size)
+                    product[slot, o, b, to, cols] = (
+                        product[slot, o, b, to, cols] + got[slot, o, i, r, cols]
+                    )
+
+                by_rows(96, 8, add)
+                first[k][o][4 + i].start()
+
+    def turn(k):
+        slot, width = k % 2, CHUNKS[k][3]
+        cols = pl.ds(0, width)
+        for o in range(2):
+            for base, i, j in ((0, 3, 4), (96, 2, 5)):
+                first[k][o][i].wait_recv()
+                first[k][o][j].wait_recv()
+            b = place1[o]
+            for q in range(4):
+                for h in range(2):
+                    row = 48 * q + 24 * h
+                    i, j, at = (3, 4, row) if row < 96 else (2, 5, row - 96)
+
+                    def add(r, o=o, b=b, q=q, h=h, row=row, i=i, j=j, at=at):
+                        mine = pl.ds(pl.multiple_of(r.start + row, 8), r.size)
+                        theirs = pl.ds(pl.multiple_of(r.start + at, 8), r.size)
+                        passed[slot, o, q, h, r, cols] = (
+                            product[slot, o, b, mine, cols]
+                            + got[slot, o, i, theirs, cols]
+                            + got[slot, o, j, theirs, cols]
+                        )
+
+                    by_rows(24, 8, add)
+            if k >= 2:
+                for d in ((YP, YM), (XP, XM))[o]:
+                    pl.semaphore_wait(credit2.at[d], 1)
+            for i in range(4):
+                second[k][o][i].start()
+        if k + 2 < count:
+            for d in range(4):
+                pl.semaphore_signal(
+                    credit.at[OPPOSITE[d]], inc=1, device_id=around[d], device_id_type=MESH
+                )
+
+    def relay2(k):
+        slot, width = k % 2, CHUNKS[k][3]
+        cols = pl.ds(0, width)
+        for o in range(2):
+            for i, shift in ((0, 1), (1, 3)):
+                second[k][o][i].wait_recv()
+                b = lax.rem(place2[o] + shift, 4)
+                passed[slot, o, b, i, :, cols] = (
+                    passed[slot, o, b, i, :, cols] + got2[slot, o, i, :, cols]
+                )
+                second[k][o][4 + i].start()
+
+    def turn2(k):
+        slot, width = k % 2, CHUNKS[k][3]
+        cols = pl.ds(0, width)
+        for o in range(2):
+            b = place2[o]
+            for h, i, j in ((0, 3, 4), (1, 2, 5)):
+                second[k][o][i].wait_recv()
+                second[k][o][j].wait_recv()
+                keep[slot, o, h, :, cols] = (
+                    passed[slot, o, b, h, :, cols]
+                    + got2[slot, o, i, :, cols]
+                    + got2[slot, o, j, :, cols]
+                )
+        if k >= 2:
+            pl.semaphore_wait(credit3, 1)
+        for o in range(2):
+            third[k][o].start()
+        if k + 2 < count:
+            for d in range(4):
+                pl.semaphore_signal(
+                    credit2.at[OPPOSITE[d]], inc=1, device_id=around[d], device_id_type=MESH
+                )
+        for o in range(2):
+            for copy in second[k][o]:
+                copy.wait_send()
+
+    def finish(k):
+        slot, (_, _, start, width, which) = k % 2, CHUNKS[k]
+        cols = pl.ds(0, width)
+        for o in range(2):
+            third[k][o].wait_recv()
+            grads[which][pl.ds(24 * o, 24), pl.ds(start, width)] = (
+                keep[slot, o, z_lo, :, cols] + got3[slot, o, :, cols]
+            )
+            third[k][o].wait_send()
+        if k + 2 < count:
+            pl.semaphore_signal(credit3, inc=1, device_id=beside, device_id_type=MESH)
+
+    parts = (dh1_part, ffn_part)
+    loads = [pltpu.make_async_copy(parts[a].at[core], sum_own.at[a], load_sem.at[a]) for a in range(2)]
+    near = [
+        remote(parts[a].at[1 - core], sum_near.at[a], sum_s.at[a, 0], sum_r.at[a, 0], mate)
+        for a in range(2)
+    ]
+    far = [
+        remote(sum_own.at[a], sum_far.at[a], sum_s.at[a, 1], sum_r.at[a, 1], across)
+        for a in range(2)
+    ]
+    back = [
+        remote(sum_near.at[a], sum_back.at[a], sum_s.at[a, 2], sum_r.at[a, 2], mate)
+        for a in range(2)
+    ]
+
+    def sum_begin(a):
+        loads[a].start()
+        near[a].start()
+
+    def sum_cross(a):
+        loads[a].wait()
+        near[a].wait_recv()
+
+        def add(r):
+            sum_own[a, r] = sum_own[a, r] + sum_near[a, r]
+
+        by_rows(HALF, 16, add)
+        far[a].start()
+
+    def tokens_end():
+        far[0].wait_recv()
+        small[0, pl.ds(24, 8), :] = jnp.zeros((8, 128), F32)
+
+        def norm(r, acc):
+            value = tokens[core, r].astype(F32)
+            total = sum_own[0, r] + sum_far[0, r]
+            inverse = lax.rsqrt(jnp.mean(value * value, axis=-1, keepdims=True) + EPSILON)
+            scaled = total * gain[...]
+            grad = (
+                dx1[r]
+                + inverse * scaled
+                - value * inverse**3 * jnp.mean(scaled * value, axis=-1, keepdims=True)
+            )
+            dg = total * value * inverse
+            low = grad.astype(BF16)
+            grad_tokens[core, r] = low
+            sum_near[0, r] = low.astype(F32)
+            return acc + dg[0:8] + dg[8:16]
+
+        def body(i, acc):
+            return norm(pl.ds(pl.multiple_of(i * 16, 16), 16), acc)
+
+        acc = lax.fori_loop(0, HALF // 16, body, jnp.zeros((8, WIDTH), F32))
+        back[0].start()
+        row = jnp.sum(acc, axis=0, keepdims=True) * 0.5
+        for i in range(12):
+            small[0, pl.ds(1 + i, 1), :] = row[:, 128 * i : 128 * i + 128]
+        small[0, pl.ds(0, 1), :] = small_in[pl.ds(0, 1), :]
+        for i in range(13, 32):
+            small[0, pl.ds(i, 1), :] = small_in[pl.ds(i, 1), :]
+
+    def out_end():
+        far[1].wait_recv()
+
+        def add(r):
+            low = (x1[r] + (sum_own[1, r] + sum_far[1, r])).astype(BF16)
+            block_out[core, r] = low
+            sum_near[1, r] = low.astype(F32)
+
+        by_rows(HALF, 16, add)
+        back[1].start()
+
+    def sum_end(a):
+        result = (grad_tokens, block_out)[a]
+        back[a].wait_recv()
+
+        def add(r):
+            result[1 - core, r] = sum_back[a, r].astype(BF16)
+
+        by_rows(HALF, 16, add)
+        for copy in (near[a], far[a], back[a]):
+            copy.wait_send()
+
+    spots = (x, y, z, core)
+    small_copies = []
+    for p in range(4):
+        small_copies.append(
+            [
+                remote(
+                    small.at[p],
+                    small_got.at[p, spots[p]],
+                    small_s.at[p, i],
+                    small_r.at[p, i],
+                    partner,
+                )
+                for i, partner in enumerate(ring[p])
+            ]
+        )
+
+    def small_begin(p):
+        for copy in small_copies[p]:
+            copy.start()
+        small_got[p, spots[p]] = small[p]
+
+    def small_end(p):
+        for copy in small_copies[p]:
+            copy.wait_recv()
+        total = small_got[p, 0] + small_got[p, 1]
+        if p < 3:
+            total = total + small_got[p, 2] + small_got[p, 3]
+            small[p + 1] = total
+        else:
+            small_out[...] = total
+        for copy in small_copies[p]:
+            copy.wait_send()
+
+    jobs = {
+        0: [lambda: sum_begin(0)],
+        1: [lambda: sum_cross(0), lambda: sum_begin(1)],
+        3: [tokens_end, lambda: sum_cross(1), lambda: small_begin(0)],
+        4: [lambda: sum_end(0), lambda: small_end(0), lambda: small_begin(1)],
+        5: [lambda: small_end(1), lambda: small_begin(2), out_end],
+        6: [lambda: small_end(2), lambda: small_begin(3), lambda: sum_end(1)],
+        7: [lambda: small_end(3)],
+    }
+
+    left_copies[0].start()
+    right_copies[0].start()
+    for k in range(count + 3):
+        if k < count:
+            multiply(k)
+        for job in jobs.get(k, ()):
+            job()
+        if 0 <= k - 1 < count:
+            turn(k - 1)
+        if k < count:
+            relay(k)
+        if 0 <= k - 2 < count:
+            turn2(k - 2)
+        if 0 <= k - 1 < count:
+            relay2(k - 1)
+        if 0 <= k - 3 < count:
+            finish(k - 3)
+    for k in (count - 2, count - 1):
+        for o in range(2):
+            for copy in first[k][o]:
+                copy.wait_send()
+
+
+def scatter(lefts, rights, ffn_part, dh1_part, x1, dx1, tokens, gain, small_in):
+    vmem = pl.BlockSpec(memory_space=pltpu.VMEM)
+    anywhere = pl.BlockSpec(memory_space=pl.ANY)
+    dma = pltpu.SemaphoreType.DMA
+    outs = pl.pallas_call(
+        scatter_kernel,
+        out_shape=tuple(jax.ShapeDtypeStruct((48, width), F32) for width in WIDTHS)
+        + (
+            jax.ShapeDtypeStruct((2, HALF, WIDTH), BF16),
+            jax.ShapeDtypeStruct((2, HALF, WIDTH), BF16),
+            jax.ShapeDtypeStruct((32, 128), F32),
+        ),
+        in_specs=[anywhere] * 10 + [vmem] * 5,
+        out_specs=(vmem,) * 7,
+        scratch_shapes=[
+            pltpu.VMEM((2, WIDTH, TOK), BF16),
+            pltpu.VMEM((2, TOK, CMAX), BF16),
+            pltpu.VMEM((2, 2, 4, 192, CMAX), F32),
+            pltpu.VMEM((2, 2, 6, 96, CMAX), F32),
+            pltpu.VMEM((2, 2, 4, 2, 24, CMAX), F32),
+            pltpu.VMEM((2, 2, 6, 24, CMAX), F32),
+            pltpu.VMEM((2, 2, 2, 24, CMAX), F32),
+            pltpu.VMEM((2, 2, 24, CMAX), F32),
+            pltpu.VMEM((2, HALF, WIDTH), F32),
+            pltpu.VMEM((2, HALF, WIDTH), F32),
+            pltpu.VMEM((2, HALF, WIDTH), F32),
+            pltpu.VMEM((2, HALF, WIDTH), F32),
+            pltpu.VMEM((4, 32, 128), F32),
+            pltpu.VMEM((4, 4, 32, 128), F32),
+            dma((2,)),
+            dma((2,)),
+            dma((2, 2, 6)),
+            dma((2, 2, 6)),
+            dma((2, 2, 6)),
+            dma((2, 2, 6)),
+            dma((2, 2)),
+            dma((2, 2)),
+            pltpu.SemaphoreType.REGULAR((4,)),
+            pltpu.SemaphoreType.REGULAR((4,)),
+            pltpu.SemaphoreType.REGULAR,
+            dma((2,)),
+            dma((2, 3)),
+            dma((2, 3)),
+            dma((4, 3)),
+            dma((4, 3)),
+        ],
+        compiler_params=pltpu.CompilerParams(
+            collective_id=0, has_side_effects=True, vmem_limit_bytes=60 * MIB
+        ),
+        name="scatter",
+    )(
+        *lefts,
+        *rights,
+        ffn_part.reshape(2, HALF, WIDTH),
+        dh1_part.reshape(2, HALF, WIDTH),
+        x1,
+        dx1,
+        tokens.reshape(2, HALF, WIDTH),
+        gain.reshape(1, WIDTH),
+        small_in,
+    )
+    return outs
 
 
 def per_device(
@@ -120,39 +826,22 @@
     )
     mixed_low = mixed.reshape(token_count, heads_local * HEAD_SIZE).astype(jnp.bfloat16)
     attn_part = jnp.dot(mixed_low, w_out, preferred_element_type=jnp.float32)
-    attention = lax.psum(attn_part, "tensor")
-    resid = tokens_f + attention
-    hidden_two, inv_two = norm_rows(resid, norm_two)
-    hidden_two_low = hidden_two.astype(jnp.bfloat16)
+    x1, hidden_two_low = attention_sum(attn_part, tokens, norm_two)
     gate = jnp.dot(hidden_two_low, w_gate, preferred_element_type=jnp.float32)
     upper = jnp.dot(hidden_two_low, w_up, preferred_element_type=jnp.float32)
     sigmoid_gate = jax.nn.sigmoid(gate)
     silu_gate = gate * sigmoid_gate
     activ_low = (silu_gate * upper).astype(jnp.bfloat16)
     ffn_part = jnp.dot(activ_low, w_down, preferred_element_type=jnp.float32)
-    feed = lax.psum(ffn_part, "tensor")
-    block_out = (resid + feed).astype(jnp.bfloat16)
-    grad_y = cotangent.astype(jnp.float32)
-    grad_down = jnp.einsum("tf,td->fd", activ_low, cotangent, preferred_element_type=jnp.float32)
     grad_activ = jnp.einsum("td,fd->tf", cotangent, w_down, preferred_element_type=jnp.float32)
     grad_gate_in = (grad_activ * upper * sigmoid_gate * (1.0 + gate * (1.0 - sigmoid_gate))).astype(
         jnp.bfloat16
     )
     grad_up_in = (grad_activ * silu_gate).astype(jnp.bfloat16)
-    grad_gate = jnp.einsum(
-        "td,tf->df", hidden_two_low, grad_gate_in, preferred_element_type=jnp.float32
-    )
-    grad_up = jnp.einsum(
-        "td,tf->df", hidden_two_low, grad_up_in, preferred_element_type=jnp.float32
-    )
     hidden_two_part = jnp.einsum(
         "tf,df->td", grad_gate_in, w_gate, preferred_element_type=jnp.float32
     ) + jnp.einsum("tf,df->td", grad_up_in, w_up, preferred_element_type=jnp.float32)
-    grad_hidden_two = lax.psum(hidden_two_part, "tensor")
-    resid_back, grad_norm_two = norm_back(resid, inv_two, norm_two, grad_hidden_two)
-    grad_resid = grad_y + resid_back
-    grad_attn_low = grad_resid.astype(jnp.bfloat16)
-    grad_out = jnp.einsum("ta,td->ad", mixed_low, grad_attn_low, preferred_element_type=jnp.float32)
+    dx1, grad_attn_low, norm_two_part = hidden_sum(hidden_two_part, x1, cotangent, norm_two)
     grad_mixed = jnp.einsum("td,ad->ta", grad_attn_low, w_out, preferred_element_type=jnp.float32)
     grad_mixed_low = grad_mixed.astype(jnp.bfloat16).reshape(
         sequence_count, sequence_length, groups_local, group_count, HEAD_SIZE
@@ -192,15 +881,6 @@
         jnp.bfloat16
     )
     grad_key_low = grad_key_raw.reshape(token_count, groups_local * HEAD_SIZE).astype(jnp.bfloat16)
-    grad_query = jnp.einsum(
-        "td,tc->dc", hidden_one_low, grad_query_low, preferred_element_type=jnp.float32
-    )
-    grad_key = jnp.einsum(
-        "td,tc->dc", hidden_one_low, grad_key_low, preferred_element_type=jnp.float32
-    )
-    grad_value = jnp.einsum(
-        "td,tc->dc", hidden_one_low, grad_values_low, preferred_element_type=jnp.float32
-    )
     hidden_one_part = (
         jnp.einsum("tc,dc->td", grad_query_low, w_query, preferred_element_type=jnp.float32)
         + jnp.einsum("tc,dc->td", grad_key_low, key_projection, preferred_element_type=jnp.float32)
@@ -208,45 +888,42 @@
             "tc,dc->td", grad_values_low, value_projection, preferred_element_type=jnp.float32
         )
     )
-    grad_hidden_one = lax.psum(hidden_one_part, "tensor")
-    tokens_back, grad_norm_one = norm_back(tokens_f, inv_one, norm_one, grad_hidden_one)
-    grad_tokens = (grad_resid + tokens_back).astype(jnp.bfloat16)
-    (
-        grad_query_sh,
-        grad_key_sh,
-        grad_value_sh,
-        grad_out_sh,
-        grad_norm_one_sh,
-        grad_gate_sh,
-        grad_up_sh,
-        grad_down_sh,
-        grad_norm_two_sh,
-    ) = (
-        lax.psum_scatter(grad_query, "dp", scatter_dimension=0, tiled=True),
-        lax.psum_scatter(grad_key, "dp", scatter_dimension=0, tiled=True),
-        lax.psum_scatter(grad_value, "dp", scatter_dimension=0, tiled=True),
-        lax.psum_scatter(grad_out, "dp", scatter_dimension=1, tiled=True),
-        lax.psum_scatter(grad_norm_one, "dp", scatter_dimension=0, tiled=True),
-        lax.psum_scatter(grad_gate, "dp", scatter_dimension=0, tiled=True),
-        lax.psum_scatter(grad_up, "dp", scatter_dimension=0, tiled=True),
-        lax.psum_scatter(grad_down, "dp", scatter_dimension=1, tiled=True),
-        lax.psum_scatter(grad_norm_two, "dp", scatter_dimension=0, tiled=True),
-    )
-    grad_q_gain, grad_k_gain = lax.psum((grad_q_part, grad_k_part), ("dp", "tensor"))
+    small_in = jnp.concatenate(
+        [
+            jnp.concatenate([grad_q_part, grad_k_part]).reshape(1, 128),
+            jnp.zeros((12, 128), F32),
+            (jnp.sum(norm_two_part, axis=0) * 0.5).reshape(12, 128),
+            jnp.zeros((7, 128), F32),
+        ],
+        axis=0,
+    )
+    lefts = (hidden_two_low.T, hidden_one_low.T, grad_attn_low.T, cotangent.T)
+    rights = (
+        jnp.concatenate([grad_gate_in, grad_up_in], axis=1),
+        jnp.concatenate([grad_query_low, grad_key_low, grad_values_low], axis=1),
+        mixed_low,
+        jnp.pad(activ_low, ((0, 0), (0, 64))),
+    )
+    gate_up, qkv, out, down, block_out, grad_tokens, small = scatter(
+        lefts, rights, ffn_part, hidden_one_part, x1, dx1, tokens, norm_one, small_in
+    )
+    norms = lax.dynamic_slice_in_dim(
+        small[1:25].reshape(2, WIDTH), lax.axis_index("dp") * 48, 48, axis=1
+    )
     return (
-        block_out,
-        grad_tokens,
-        grad_norm_one_sh,
-        grad_query_sh,
-        grad_key_sh,
-        grad_value_sh,
-        grad_out_sh,
-        grad_q_gain,
-        grad_k_gain,
-        grad_norm_two_sh,
-        grad_gate_sh,
-        grad_up_sh,
-        grad_down_sh,
+        block_out.reshape(TOK, WIDTH),
+        grad_tokens.reshape(TOK, WIDTH),
+        norms[0],
+        qkv[:, :384],
+        qkv[:, 384:512],
+        qkv[:, 512:640],
+        out.T,
+        small[0, :64],
+        small[0, 64:],
+        norms[1],
+        gate_up[:, :FFL],
+        gate_up[:, FFL:],
+        down[:, :FFL].T,
     )
 
 

time: 1760 us -> 477 us (0.27)
  waiting for transfers between devices: 1340 us -> 0 us
  Pallas kernels: 0 us -> 303 us
  blocking collectives: 246 us -> 0 us
  local copies, waits for them, and re-layouts: 28.3 us -> 66.1 us
  matrix products: 86.1 us -> 67.4 us
    reduce_scatter x7 -> x0, waiting for transfers between devices: 1200 us -> none  [the longest x1 245 us: per_device(): lax.psum_scatter(grad_up, 'dp', scatter_dimension=0, tiled=True)]
    pallas_call x0 -> x3, Pallas kernels: none -> 303 us  [the longest x1 219 us: scatter(): pl.pallas_call(scatter_kernel, out_shape=tuple((jax.ShapeDtypeStruct((48,...]
    unnamed x1 -> x0, blocking collectives: 154 us -> none
    psum x3 -> x0, waiting for transfers between devices: 140 us -> none  [the longest x1 78.1 us: per_device(): attention = lax.psum(attn_part, 'tensor')]
    psum x1 -> x0, blocking collectives: 91.6 us -> none  [per_device(): lax.psum((grad_q_part, grad_k_part), ('dp', 'tensor'))]
    dot_general x7 -> x0, matrix products: 32.9 us -> none  [the longest x1 7.61 us: per_device(): jnp.einsum('td,tf->df', hidden_two_low, grad_up_in, preferred_element_typ...]
  transfers between devices with their start and end apart: 10 -> 0, of which waited for: 8 -> 0; matrix products, arithmetic and copies ran while one was open for 4% -> 0% of each run, Pallas kernels for 0% -> 0%
where the time goes in v1:
time: 477 us; the launch traced here: 469 us
  Pallas kernels  303 us (64%)
  matrix products  67.4 us (14%)
  local copies, waits for them, and re-layouts  66.1 us (14%)
  other arithmetic  29.9 us (6%)
    pallas_call x1, Pallas kernels, scatter(): pl.pallas_call(scatter_kernel, out_shape=tuple((jax.ShapeDtypeStruct((48,...  219 us
    pallas_call x1, Pallas kernels, attention_sum(): pl.pallas_call(start_norm_kernel, out_shape=(jax.ShapeDtypeStruct((HALF,...  42.6 us
    pallas_call x1, Pallas kernels, hidden_sum(): pl.pallas_call(back_norm_kernel, out_shape=(jax.ShapeDtypeStruct((HALF, W...  42.3 us
    unnamed x137, local copies, waits for them, and re-layouts  11 us

profile of v1, /device:TPU:0, one launch (start us, length us, event | category | flops | bytes accessed | tf_op | source)
XLA Modules:
  0.0 468.9 jit_solution(5652026000326109181)
XLA Ops:
  3.0 2.4 fusion.46
  20.3 2.7 fusion.18
  24.9 2.0 fusion.21.part
  27.0 42.6 %attention_sum.1 = (f32[256,1536]{1,0:T(8,128)S(1)}, bf16[2,256,1536]{2,1,0:T(8,128)(2,1)S(1)}) custom-call(f32[2,256,1536]{2,1,0:T(8,128)S(1)} %fusion.21.part, bf16[2,256,1536]{2,1,0:T(8,128)(2,1)S(1)} %bitcast.191, f32[1,1536]{1,0:T(1,128)S(1)} %reshape.707.gain), custom_call_target="tpu_custom_call" | custom-call | tf_op jit(solution)/shard_map/attention_sum/pallas_call | solution.py:181
  69.6 6.7 %fusion.54 = f32[512,1728]{1,0:T(8,128)S(1)} fusion(bf16[512,1536]{1,0:T(8,128)(2,1)S(1)} %bitcast.194, bf16[1536,1728]{0,1:T(8,128)(2,1)} %param.24), kind=kOutput, calls=%fused_computation.110 | convolution fusion | flops 2717908992 | bytes 10420224 | tf_op jit(solution)/shard_map/dot_general | solution.py:830
  76.3 4.9 %fusion.53 = f32[512,1728]{1,0:T(8,128)} fusion(bf16[512,1536]{1,0:T(8,128)(2,1)S(1)} %copy-done.4, bf16[1728,1536]{1,0:T(8,128)(2,1)S(1)} %bitcast.237), kind=kOutput, calls=%fused_computation.109 | convolution fusion | flops 2717908992 | bytes 10420224 | tf_op jit(solution)/shard_map/td,fd->tf/dot_general | solution.py:836
  81.3 8.3 %multiply_convert_fusion = (bf16[512,1728]{1,0:T(8,128)(2,1)}, bf16[512,1728]{1,0:T(8,128)(2,1)S(1)}, bf16[512,1728]{1,0:T(8,128)(2,1)S(1)}) fusion(f32[512,1728]{1,0:T(8,128)S(1)} %fusion.54, f32[512,1728]{1,0:T(8,128)} %fusion.53, bf16[512,1536]{1,0:T(8,128)(2,1)S(1)} %bitcast.195, bf16[1536,1728]{0,1:T(8,128)(2,1)} %param.25), kind=kOutput, calls=%fused_computation.12 | convolution fusion | flops 2731180032 | bytes 19267584 | tf_op jit(solution)/shard_map/dot_general | solution.py:831
  89.6 6.4 %fusion.55 = f32[512,1536]{1,0:T(8,128)S(1)} fusion(bf16[512,1728]{1,0:T(8,128)(2,1)S(1)} %get-tuple-element.38, bf16[1536,1728]{0,1:T(8,128)(2,1)} %param.24), kind=kOutput, calls=%fused_computation.111 | convolution fusion | flops 2717908992 | bytes 10223616 | tf_op jit(solution)/shard_map/tf,df->td/dot_general | solution.py:841
  96.0 5.2 %convolution_add_fusion.2 = f32[512,1536]{1,0:T(8,128)S(1)} fusion(f32[512,1536]{1,0:T(8,128)S(1)} %fusion.55, bf16[512,1728]{1,0:T(8,128)(2,1)S(1)} %get-tuple-element.39, bf16[1536,1728]{0,1:T(8,128)(2,1)} %param.25), kind=kOutput, calls=%fused_computation.20 | convolution fusion | flops 2718695424 | bytes 13369344 | tf_op jit(solution)/shard_map/tf,df->td/dot_general | solution.py:843
  101.2 42.3 %hidden_sum.1 = (f32[256,1536]{1,0:T(8,128)S(1)}, bf16[2,256,1536]{2,1,0:T(8,128)(2,1)S(1)}, f32[8,1536]{1,0:T(8,128)S(1)}) custom-call(f32[2,256,1536]{2,1,0:T(8,128)S(1)} %bitcast.193, f32[256,1536]{1,0:T(8,128)S(1)} %get-tuple-element.26.x1.refs_10_, bf16[2,256,1536]{2,1,0:T(8,128)(2,1)S(1)} %bitcast.192, f32[1,1536]{1,0:T(1,128)S(1)} %reshape.707.gain), custom_call_target="tpu_custom_call" | custom-call | tf_op jit(solution)/shard_map/hidden_sum/pallas_call | solution.py:267
  144.6 2.3 fusion
  146.9 2.2 fusion.10
  153.8 2.6 concatenate.104
  158.3 2.6 concatenate.105
  164.2 2.5 reshape.717
  166.7 3.9 fusion.17
  186.0 2.4 copy.114
  189.5 2.3 copy.115
  192.8 2.4 copy.117
  195.2 2.1 subtract_convert_fusion
  197.5 2.7 fusion.57
  201.1 2.6 convolution_add_fusion.1
  203.8 4.7 fusion.28
  208.5 2.3 convolution_add_fusion
  211.9 4.7 pad_maximum_fusion.refs_4_
  216.5 2.8 copy.149
  219.4 7.9 %fusion.56 = f32[512,1536]{1,0:T(8,128)} fusion(bf16[512,1728]{1,0:T(8,128)(2,1)} %get-tuple-element.37, bf16[1728,1536]{1,0:T(8,128)(2,1)} %param.26), kind=kOutput, calls=%fused_computation.112 | convolution fusion | flops 2717908992 | bytes 10223616 | tf_op jit(solution)/shard_map/dot_general | solution.py:835
  228.6 2.6 copy.148
  232.2 3.0 fusion.45.refs_1_
  237.3 218.6 %scatter.1 = (f32[48,3456]{1,0:T(8,128)}, f32[48,640]{1,0:T(8,128)}, f32[48,384]{1,0:T(8,128)}, f32[48,1792]{1,0:T(8,128)}, bf16[2,256,1536]{2,1,0:T(8,128)(2,1)...) custom-call(bf16[1536,512]{1,0:T(8,128)(2,1)} %bitcast.206, bf16[1536,512]{1,0:T(8,128)(2,1)} %fusion.45.refs_1_, ...), custom_call_target="tpu_custom_call" | custom-call | tf_op jit(solution)/shard_map/scatter/pallas_call | solution.py:707
  456.0 2.4 fusion.51
  463.9 2.8 copy.155
  (223 shorter events, 61.0 us)
Async XLA Ops:
  0.6 24.3 %copy-start = (bf16[384,1536]{1,0:T(8,128)(2,1)S(1)}, bf16[384,1536]{1,0:T(8,128)(2,1)}, u32[]{:S(2)}) copy-start(bf16[384,1536]{1,0:T(8,128)(2,1)} %param.20) | copy-start | bytes 3538948
  2.5 16.5 %copy-start.11 = (bf16[512,1536]{0,1:T(8,128)(2,1)}, bf16[512,1536]{0,1:T(8,128)(2,1)S(1)}, u32[]{:S(2)}) copy-start(bf16[512,1536]{0,1:T(8,128)(2,1)S(1)} %copy.101) | copy-start | bytes 4718596
  11.5 4.4 copy-start.55
  13.5 4.1 copy-start.31
  13.5 4.1 copy-start.33
  16.4 130.5 %copy-start.15 = (pred[512,512]{0,1:T(8,128)(4,1)}, pred[512,512]{0,1:T(8,128)(4,1)S(1)}, u32[]{:S(2)}) copy-start(pred[512,512]{0,1:T(8,128)(4,1)S(1)} %fusion.31) | copy-start | bytes 786436
  17.6 129.3 %copy-start.38 = (f32[2,3,512]{2,1,0:T(4,128)}, f32[2,3,512]{2,1,0:T(4,128)S(1)}, u32[]{:S(2)}) copy-start(f32[2,3,512]{2,1,0:T(4,128)S(1)} %get-tuple-element.66) | copy-start | bytes 36868
  19.0 127.9 %copy-start.40 = (f32[2,3,512]{2,1,0:T(4,128)}, f32[2,3,512]{2,1,0:T(4,128)S(1)}, u32[]{:S(2)}) copy-start(f32[2,3,512]{2,1,0:T(4,128)S(1)} %fusion.4) | copy-start | bytes 36868
  23.0 4.0 copy-start.49
  23.0 4.0 copy-start.2
  27.0 49.3 %slice-start.2 = ((s8[5308416]{0:T(1024)(128)(4,1)}), s8[4194304]{0:T(1024)(128)(4,1)S(1)}, s32[]{:S(2)}) async-start(s8[5308416]{0:T(1024)(128)(4,1)} %bitcast.236), calls=%async_computation.2 | async-start | bytes 8388608
  69.6 11.7 %copy-start.6 = (bf16[2,256,1536]{2,1,0:T(8,128)(2,1)}, bf16[2,256,1536]{2,1,0:T(8,128)(2,1)S(1)}, u32[]{:S(2)}) copy-start(bf16[2,256,1536]{2,1,0:T(8,128)(2,1)S(1)} %get-tuple-element.25) | copy-start | bytes 4718596
  69.6 31.6 %copy-start.3 = (f32[256,1536]{1,0:T(8,128)}, f32[256,1536]{1,0:T(8,128)S(1)}, u32[]{:S(2)}) copy-start(f32[256,1536]{1,0:T(8,128)S(1)} %get-tuple-element.26.x1.refs_10_) | copy-start | bytes 4718596
  69.6 6.7 %copy-start.4 = (bf16[512,1536]{1,0:T(8,128)(2,1)S(1)}, bf16[512,1536]{1,0:T(8,128)(2,1)}, u32[]{:S(2)}) copy-start(bf16[512,1536]{1,0:T(8,128)(2,1)} %param.27) | copy-start | bytes 4718596
  69.6 6.7 %slice-start.3 = ((s8[5308416]{0:T(1024)(128)(4,1)}), s8[1114112]{0:T(1024)(128)(4,1)S(1)}, s32[]{:S(2)}) async-start(s8[5308416]{0:T(1024)(128)(4,1)} %bitcast.236), calls=%async_computation.3 | async-start | bytes 2228224
  89.6 6.4 %copy-start.18 = (bf16[512,1728]{1,0:T(8,128)(2,1)}, bf16[512,1728]{1,0:T(8,128)(2,1)S(1)}, u32[]{:S(2)}) copy-start(bf16[512,1728]{1,0:T(8,128)(2,1)S(1)} %get-tuple-element.38) | copy-start | bytes 5308420
  89.6 6.4 %copy-start.19 = (bf16[512,1728]{1,0:T(8,128)(2,1)}, bf16[512,1728]{1,0:T(8,128)(2,1)S(1)}, u32[]{:S(2)}) copy-start(bf16[512,1728]{1,0:T(8,128)(2,1)S(1)} %get-tuple-element.39) | copy-start | bytes 5308420
  89.6 54.7 %slice-start = ((s8[6291456]{0:T(1024)(128)(4,1)}), s8[4194304]{0:T(1024)(128)(4,1)S(1)}, s32[]{:S(2)}) async-start(s8[6291456]{0:T(1024)(128)(4,1)} %bitcast.199), calls=%async_computation | async-start | bytes 8388608
  96.0 48.3 %slice-start.1 = ((s8[6291456]{0:T(1024)(128)(4,1)}), s8[2097152]{0:T(1024)(128)(4,1)S(1)}, s32[]{:S(2)}) async-start(s8[6291456]{0:T(1024)(128)(4,1)} %bitcast.199), calls=%async_computation.1 | async-start | bytes 4194304
  156.4 6.6 %copy-start.13 = (f32[512,384]{0,1:T(8,128)S(1)}, f32[512,384]{0,1:T(8,128)}, u32[]{:S(2)}) copy-start(f32[512,384]{0,1:T(8,128)} %copy-done.12) | copy-start | bytes 2359300
  166.7 5.0 %copy-start.25 = (f32[512,32]{0,1:T(8,128)S(1)}, f32[512,32]{0,1:T(8,128)}, u32[]{:S(2)}) copy-start(f32[512,32]{0,1:T(8,128)} %copy-done.23) | copy-start | bytes 196612
  171.7 11.1 %copy-start.57 = (f32[64]{0:T(128)S(1)}, f32[64]{0:T(128)}, u32[]{:S(2)}) copy-start(f32[64]{0:T(128)} %fusion.17) | copy-start | bytes 772
  171.7 12.0 %copy-start.54 = (f32[64]{0:T(128)S(1)}, f32[64]{0:T(128)}, u32[]{:S(2)}) copy-start(f32[64]{0:T(128)} %param.21) | copy-start | bytes 772
  184.8 7.0 %copy-start.42 = (f32[512,6]{0,1:T(8,128)S(1)}, f32[512,6]{0,1:T(8,128)}, u32[]{:S(2)}) copy-start(f32[512,6]{0,1:T(8,128)} %get-tuple-element.58) | copy-start | bytes 36868
  186.0 9.2 %copy-start.14 = (f32[512,384]{1,0:T(8,128)S(1)}, f32[512,384]{1,0:T(8,128)}, u32[]{:S(2)}) copy-start(f32[512,384]{1,0:T(8,128)} %copy.116) | copy-start | bytes 2359300
  203.8 4.7 %copy-start.36 = (bf16[1536,128]{1,0:T(8,128)(2,1)S(1)}, bf16[1536,128]{1,0:T(8,128)(2,1)}, u32[]{:S(2)}) copy-start(bf16[1536,128]{1,0:T(8,128)(2,1)} %param.19) | copy-start | bytes 1179652
  219.4 7.9 %copy-start.20 = (bf16[512,1728]{1,0:T(8,128)(2,1)S(1)}, bf16[512,1728]{1,0:T(8,128)(2,1)}, u32[]{:S(2)}) copy-start(bf16[512,1728]{1,0:T(8,128)(2,1)} %get-tuple-element.37) | copy-start | bytes 5308420
  227.3 4.0 copy-start.27
  227.3 4.9 %copy-start.45 = (f32[1536]{0:T(1024)S(1)}, f32[1536]{0:T(1024)}, u32[]{:S(2)}) copy-start(f32[1536]{0:T(1024)} %param.16) | copy-start | bytes 18436
  227.3 4.9 %copy-start.52 = (f32[512]{0:T(512)S(1)}, f32[512]{0:T(512)}, u32[]{:S(2)}) copy-start(f32[512]{0:T(512)} %copy-done.50) | copy-start | bytes 6148
  455.9 10.7 %copy-start.26 = (bf16[2,256,1536]{2,1,0:T(8,128)(2,1)S(1)}, bf16[2,256,1536]{2,1,0:T(8,128)(2,1)}, u32[]{:S(2)}) copy-start(bf16[2,256,1536]{2,1,0:T(8,128)(2,1)} %get-tuple-element.31) | copy-start | bytes 4718596
  463.9 4.5 copy-start.1
  (34 other events, 88.6 us)
